TPU v7x, 128 devices: a whole 4x4x4 slice. The times are simulated.
128 devices in a mesh: ocn: 32 (over y, x, core), col: 4 (over z).
Axes of the slice: x: 4, y: 4, z: 4, core: 2. Of those that a mesh axis runs over, the one named last changes fastest.
Arguments:
- air_flux: float32 [8, 262144], P(None, ('ocn', 'col')), may hold values from -6 to 6
- send_index: int32 [128, 128, 16], P(('ocn', 'col')), may hold values from 0 to 2047
- remap_column: int32 [4, 262144], P(None, ('ocn', 'col')), may hold values from 0 to 2047
- remap_weight: float32 [4, 262144], P(None, ('ocn', 'col')), may hold values from 0.05 to 0.5
- halo_send: int32 [128, 4, 128], P(('ocn', 'col')), may hold values from 0 to 2047
- neighbours: int32 [6, 262144], P(None, ('ocn', 'col')), may hold values from 0 to 2559
- gradient_weight: float32 [2, 6, 262144], P(None, None, ('ocn', 'col')), may hold values from -0.36 to 0.36
- coriolis: float32 [262144], P(('ocn', 'col')), may hold values from -0.25 to 0.25
- sea_surface: float32 [262144], P(('ocn', 'col')), may hold values from -3 to 3
- velocity: float32 [2, 262144], P(None, ('ocn', 'col')), may hold values from -3 to 3
- lateral_weight: float32 [6, 262144], P(None, ('ocn', 'col')), may hold values from 0.005 to 0.08
- layer_count: int32 [262144], P(('ocn', 'col')), may hold values from 16 to 64
- thickness: float32 [64, 262144], P(None, ('ocn', 'col')), may hold values from 2 to 12
- diffusivity: float32 [63, 262144], P(None, ('ocn', 'col')), may hold values from 0.02 to 20
- tracers: float32 [4, 64, 262144], P(None, None, ('ocn', 'col')), may hold values from -6 to 6
Outputs:
- mixed_tracers: float32 [4, 64, 262144], P(None, None, ('ocn', 'col'))
- final_surface: float32 [262144], P(('ocn', 'col'))
- final_velocity: float32 [2, 262144], P(None, ('ocn', 'col'))
Inputs may be any that keep to these rules, and one draw needn't show every extreme that they name: `send_index`: entry [q, r, j] is one of device q's own 2048 atmosphere cells, counted from its first. `halo_send`: entries are cells of the sending partition, counted from its first. `neighbours`: values under 2048 are the partition's own cells; the rest are halo blocks of 128 in the order of partners at offsets 1, -1, 2, -2.
All inputs are finite; a program needn't handle non-finite values.
Results may differ from a plain program's by a relative error of at most 0.00002.
Values sent between devices are 32-bit elements; how exact they have to be, the bound alone decides.
A program may use at most 128 MiB of HBM per device.

v0:
```python
import jax
import jax.numpy as jnp
from jax import lax
from jax.experimental import pallas as pl
from jax.experimental.pallas import tpu as pltpu
from jax.sharding import PartitionSpec as P

F32 = jnp.float32
BF16 = jnp.bfloat16
I32 = jnp.int32
MESH = pl.DeviceIdType.MESH

SUBCYCLES = 8
LAYERS = 64
TRACERS = 4
ROWS = TRACERS * LAYERS
EDGES = 6
BLOCKS = 16
OFFSETS = (1, -1, 2, -2)
DISTANCES = (1, -1, 2, -2, 3, -3, 4, -4)
FLUX_GAIN = 2.0
FORCE_GAIN = 0.05

NB, G0, G1, COR, VEL, FORCE, FIXED = 0, 6, 12, 18, 19, 21, 24
N_COLS = 256
K_ROWS = 1024
PIECE = 32


def wide(row):
    return jnp.broadcast_to(row, (8, 128))


def lane_pick(source, lane):
    return jnp.take_along_axis(source, lane, axis=1, mode="promise_in_bounds")


def ocean_kernel(
    ocn_size,
    col_size,
    air_hbm,
    send_hbm,
    column_hbm,
    remap_hbm,
    halo_send_hbm,
    neighbours_hbm,
    gradient_hbm,
    coriolis_hbm,
    surface_hbm,
    velocity_hbm,
    lateral_hbm,
    count_hbm,
    thick_hbm,
    diffusivity_hbm,
    tracer_hbm,
    rest_hbm,
    share_hbm,
    heads,
    final_surface,
    final_velocity,
    air,
    send_index,
    column,
    remap_weight,
    halo_lists,
    neighbours,
    gradient,
    coriolis,
    surface,
    velocity,
    lateral,
    count,
    thick,
    diffus,
    tracer,
    tab,
    square,
    outgoing,
    passing,
    arrived,
    received,
    halves,
    flux,
    list_fixed,
    ghost_fixed,
    force_out,
    force_in,
    own_lane,
    own_block,
    list_lane,
    list_block,
    list_g,
    ghost_lane,
    ghost_block,
    ghost_g,
    height,
    speed,
    ghost_rows,
    message,
    near_box,
    far_box,
    halo_out,
    halo_in,
    parts,
    halo_parts,
    total,
    profile,
    thick_cells,
    diffus_cells,
    gain_here,
    gain_below,
    gain_above,
    tops,
    load_sem,
    store_sem,
    col_send,
    col_recv,
    col_own,
    ocn_send,
    ocn_recv,
    ocn_own,
    fixed_send,
    fixed_recv,
    force_send,
    force_recv,
    halo_send_sem,
    halo_recv,
    near_send,
    near_recv,
    far_send,
    far_recv,
):
    devices = ocn_size * col_size
    ocn, col = lax.axis_index("ocn"), lax.axis_index("col")
    me = ocn * col_size + col
    odd = lax.rem(ocn, 2)

    def device(distance):
        target = lax.rem(me + (distance + devices), devices)
        return (target // col_size, lax.rem(target, col_size))

    column_size = 2 * col_size
    chips = ocn_size // 2
    chip, place_in_column = ocn // 2, odd * col_size + col

    def in_column(step):
        to = lax.rem(place_in_column + step, column_size)
        return to, (chip * 2 + to // col_size, lax.rem(to, col_size))

    def across(step):
        to = lax.rem(chip + step, chips)
        return to, (to * 2 + odd, col)

    sources = (
        air_hbm, send_hbm, halo_send_hbm, neighbours_hbm, gradient_hbm, coriolis_hbm, surface_hbm, velocity_hbm,
        tracer_hbm, column_hbm, remap_hbm, lateral_hbm, count_hbm, thick_hbm, diffusivity_hbm,
    )
    targets = (
        air, send_index, halo_lists, neighbours, gradient, coriolis, surface, velocity,
        tracer, column, remap_weight, lateral, count, thick, diffus,
    )
    loads = [
        pltpu.make_async_copy(source, target, load_sem.at[i])
        for i, (source, target) in enumerate(zip(sources, targets))
    ]
    for load in loads[:2]:
        load.start()

    barrier = pltpu.get_barrier_semaphore()
    for distance in DISTANCES:
        pl.semaphore_signal(barrier, inc=1, device_id=device(distance), device_id_type=MESH)
    for step in range(1, column_size):
        pl.semaphore_signal(barrier, inc=1, device_id=in_column(step)[1], device_id_type=MESH)
    for step in range(1, chips):
        pl.semaphore_signal(barrier, inc=1, device_id=across(step)[1], device_id_type=MESH)
    for load in loads[2:]:
        load.start()

    loads[0].wait()
    loads[1].wait()
    for slot in range(BLOCKS):
        index = wide(send_index[pl.ds(slot, 1), :])
        lane, block = index & 127, index >> 7
        got = jnp.zeros((8, 128), F32)
        for j in range(BLOCKS):
            got = jnp.where(block == j, lane_pick(air[:, pl.ds(j * 128, 128)], lane), got)
        square[pl.ds(slot, 8, stride=16), :] = got
    turned = square[...].T
    for target in range(ocn_size * col_size):
        outgoing[target // column_size, target % column_size, :, :] = turned[target : target + 1]
    pl.semaphore_wait(barrier, len(DISTANCES) + column_size - 1 + chips - 1)
    for i in range(column_size - 1):
        to, target = in_column(1 + (i + 1) % (column_size - 1))
        pltpu.make_async_remote_copy(
            outgoing.at[:, to], passing.at[place_in_column], col_send, col_recv,
            device_id=target, device_id_type=MESH,
        ).start()
    stay = pltpu.make_async_copy(outgoing.at[:, place_in_column], passing.at[place_in_column], col_own)
    stay.start()

    for load in loads[2:8]:
        load.wait()
    halo_send = halo_lists.at[0]

    for c in range(BLOCKS):
        cells = pl.ds(c * 128, 128)
        tab[pl.ds(NB * 16 + c, EDGES, stride=16), :] = neighbours[:, cells].astype(F32)
        for m in range(EDGES):
            tab[pl.ds((G0 + m) * 16 + c, 2, stride=16 * EDGES), :] = gradient[m, :, cells]
        tab[pl.ds(VEL * 16 + c, 2, stride=16), :] = velocity[:, cells]
    tab[pl.ds(COR * 16, 16), :] = coriolis[...]
    tab[pl.ds(FORCE * 16, 48), :] = jnp.zeros((48, 128), F32)
    for t in range(12):
        index = tab[pl.ds(t * 8, 8), :].astype(I32)
        own_lane[pl.ds(t * 8, 8), :] = index & 127
        own_block[pl.ds(t * 8, 8), :] = index >> 7

    gathered = passing.at[pl.ds(0, column_size - 1)]
    pltpu.make_async_copy(gathered, gathered, col_recv).wait()
    stay.wait()
    landing = arrived.at[pl.ds(chip * column_size, column_size)]
    for i in range(chips - 1):
        to, target = across(1 + (i + chips // 2 - 3) % (chips - 1))
        pltpu.make_async_remote_copy(
            passing.at[:, to], landing, ocn_send, ocn_recv, device_id=target, device_id_type=MESH
        ).start()
    stay = pltpu.make_async_copy(passing.at[:, chip], landing, ocn_own)
    stay.start()

    lists = jnp.concatenate([halo_send[...]] * 2, axis=0)
    lists_lane, lists_block = lists & 127, lists >> 7

    def list_values(load):
        got = jnp.zeros((8, 128), F32)
        for j in range(BLOCKS):
            got = jnp.where(lists_block == j, lane_pick(wide(load(j)), lists_lane), got)
        return got

    def collect(field, carry):
        got = list_values(lambda j: tab[pl.ds(field * 16 + j, 1), :])
        list_fixed[pl.ds(field, 4, stride=FIXED), :] = got[:4]
        return carry

    lax.fori_loop(0, FIXED, collect, 0, unroll=4)
    for b in range(4):
        rows = pl.ds(b * FIXED, FIXED)
        pltpu.make_async_remote_copy(
            list_fixed.at[rows], ghost_fixed.at[rows], fixed_send, fixed_recv,
            device_id=device(-OFFSETS[b]), device_id_type=MESH,
        ).start()

    def by_edge(fixed, lane_ref, block_ref, g_ref):
        for b in range(4):
            index = fixed[pl.ds(b * FIXED + NB, EDGES), :].astype(I32)
            lane_ref[pl.ds(b, EDGES, stride=4), :] = index & 127
            block_ref[pl.ds(b, EDGES, stride=4), :] = index >> 7
            g_ref[pl.ds(b, EDGES, stride=4), :] = fixed[pl.ds(b * FIXED + G0, EDGES), :]
            g_ref[pl.ds(24 + b, EDGES, stride=4), :] = fixed[pl.ds(b * FIXED + G1, EDGES), :]

    by_edge(list_fixed, list_lane, list_block, list_g)

    def merge_lateral():
        index = [neighbours[pl.ds(m, 1), :] for m in range(EDGES)]
        weight = [lateral[pl.ds(m, 1), :] for m in range(EDGES)]
        for m in range(1, EDGES):
            moved = index[m] == index[0]
            weight[0] = weight[0] + jnp.where(moved, weight[m], 0.0)
            for k in range(1, m):
                same = jnp.logical_and(index[m] == index[k], jnp.logical_not(moved))
                weight[k] = weight[k] + jnp.where(same, weight[m], 0.0)
                moved = jnp.logical_or(moved, same)
            weight[m] = jnp.where(moved, 0.0, weight[m])
        for m in range(EDGES):
            lateral[pl.ds(m, 1), :] = weight[m]

    def mix(n, first_row, source, column0, count_rows):
        cells = pl.ds(pl.multiple_of(n * N_COLS, N_COLS), N_COLS)
        row = lax.broadcasted_iota(I32, (count_rows, N_COLS), 0) + first_row
        matrix = jnp.zeros((count_rows, N_COLS), F32)
        for m in reversed(range(EDGES)):
            here = row == neighbours[pl.ds(m, 1), cells]
            matrix = jnp.where(here, lateral[pl.ds(m, 1), cells], matrix)
        high = matrix.astype(BF16)
        low = (matrix - high.astype(F32)).astype(BF16)
        values = source[:, pl.ds(column0, count_rows)]
        both = jnp.dot(values, high, preferred_element_type=F32)
        added = both[:ROWS] + both[ROWS:] + jnp.dot(values[:ROWS], low, preferred_element_type=F32)
        total[:, cells] = total[:, cells] + added

    def mix_own(n):
        total[:, pl.ds(pl.multiple_of(n * N_COLS, N_COLS), N_COLS)] = jnp.zeros((ROWS, N_COLS), F32)

        def step(k, carry):
            first = pl.multiple_of(k * K_ROWS, K_ROWS)
            mix(n, first, parts, first, K_ROWS)
            return carry

        lax.fori_loop(0, 2048 // K_ROWS, step, 0)

    def mix_halo(n):
        mix(n, 2048, halo_parts, 0, 512)
        sub = lax.broadcasted_iota(I32, (8, 128), 0)
        for part in range(2):
            c = n * 2 + part
            cells = pl.ds(pl.multiple_of(c * 128, 128), 128)
            weight = lateral[pl.ds(0, 1), cells]
            for m in range(1, EDGES):
                weight = weight + lateral[pl.ds(m, 1), cells]
            weight = wide(weight)
            layers = wide(count[pl.ds(c, 1), :])
            for g in range(ROWS // 8):
                rows = pl.ds(g * 8, 8)
                value = tracer[rows, cells]
                live = sub + (g * 8) % LAYERS < layers
                value = value + jnp.where(live, total[rows, cells] - weight * value, 0.0)
                profile[pl.ds(g * 128 + c, 8, stride=16), :] = value

    def select_halo():
        loads[8].wait()
        for t in range(TRACERS):
            rows = pl.ds(t * LAYERS, LAYERS)
            value = tracer[rows, :]
            high = value.astype(BF16)
            parts[rows, :] = high
            parts[pl.ds(ROWS + t * LAYERS, LAYERS), :] = (value - high.astype(F32)).astype(BF16)
        place = lax.broadcasted_iota(I32, (2048, 256), 0)
        for pair in range(2):
            lists = [halo_send[pl.ds(pair * 2 + b, 1), :] for b in range(2)]
            chosen = jnp.where(place == jnp.concatenate(lists, axis=1), 1.0, 0.0).astype(BF16)
            both = jnp.dot(parts[...], chosen, preferred_element_type=F32)
            both = both[:ROWS] + both[ROWS:]
            for b in range(2):
                halo_out[pair * 2 + b] = both[:, b * 128 : b * 128 + 128]

    def send_halo(t):
        rows = pl.ds(pl.multiple_of(t * LAYERS, LAYERS), LAYERS)
        for b in range(4):
            pltpu.make_async_remote_copy(
                halo_out.at[b, rows], halo_in.at[b, rows], halo_send_sem, halo_recv,
                device_id=device(-OFFSETS[b]), device_id_type=MESH,
            ).start()

    def layer(index):
        return pl.ds(pl.multiple_of(index * 16, 16), 16)

    def active(index):
        return (index < count[...]).astype(F32)

    def couple(index, upper):
        lower = thick_cells[layer(index + 1), :]
        return diffus_cells[layer(index), :] * 2.0 / (upper + lower) * active(index + 1)

    def vertical_gains():
        for load in loads[12:15]:
            load.wait()
        for c in range(BLOCKS):
            cells = pl.ds(c * 128, 128)
            for g in range(8):
                thick_cells[pl.ds(g * 128 + c, 8, stride=16), :] = thick[pl.ds(g * 8, 8), cells]
                size = 8 if g < 7 else 7
                diffus_cells[pl.ds(g * 128 + c, size, stride=16), :] = diffus[pl.ds(g * 8, size), cells]

        def step(i, carry):
            below, gain = carry
            index = LAYERS - 1 - i
            here = thick_cells[layer(index), :]
            above = couple(index - 1, thick_cells[layer(index - 1), :])
            inverse = 1.0 / (here + above + below - below * gain)
            gain_here[layer(index), :] = here * inverse
            gain_below[layer(index), :] = below * inverse
            gain = above * inverse
            gain_above[layer(index), :] = gain
            return above, gain

        zero = jnp.zeros((16, 128), F32)
        return lax.fori_loop(0, LAYERS - 2, step, (zero, zero))

    couple_one, gain_two = vertical_gains()
    loads[11].wait()
    merge_lateral()

    for load in loads[9:11]:
        load.wait()
    others = pl.ds(0, devices - column_size)
    pltpu.make_async_copy(arrived.at[others], arrived.at[others], ocn_recv).wait()
    stay.wait()
    square[...] = arrived[:, 0, :].T
    for slot in range(BLOCKS):
        received[slot] = square[pl.ds(slot, 8, stride=16), :]

    def remap(start):
        upper = lax.broadcasted_iota(I32, (8, 128), 0) < 4
        for slot in range(BLOCKS):
            tile = received[slot]
            other = pltpu.roll(tile, 4, 0)
            halves[slot] = jnp.where(upper, tile, other) if start == 0 else jnp.where(upper, other, tile)

        def step(pair, carry):
            cells = [pl.ds(pl.multiple_of(pair * 256 + half * 128, 128), 128) for half in range(2)]
            result = jnp.zeros((8, 128), F32)
            for k in range(4):
                index = jnp.where(upper, wide(column[pl.ds(k, 1), cells[0]]), wide(column[pl.ds(k, 1), cells[1]]))
                weight = jnp.where(
                    upper, wide(remap_weight[pl.ds(k, 1), cells[0]]), wide(remap_weight[pl.ds(k, 1), cells[1]])
                )
                lane, block = index >> 4, index & 15
                got = jnp.zeros((8, 128), F32)
                for j in range(BLOCKS):
                    got = jnp.where(block == j, lane_pick(halves[j], lane), got)
                result = result + weight * got
            flux[pl.ds(start * 16 + pair * 2, 4, stride=16), :] = result[:4]
            flux[pl.ds(start * 16 + pair * 2 + 1, 4, stride=16), :] = result[4:]
            return carry

        lax.fori_loop(0, BLOCKS // 2, step, 0, unroll=4)

    remap(4)
    tab[pl.ds(FORCE * 16, 32), :] = flux[pl.ds(64, 32), :]

    sub = lax.broadcasted_iota(I32, (8, 128), 0)
    forces = [list_values(lambda j, a=a: tab[pl.ds((FORCE + a) * 16 + j, 1), :]) for a in range(2)]
    force_out[...] = jnp.where(sub < 4, forces[0], forces[1])
    for b in range(4):
        pltpu.make_async_remote_copy(
            force_out, force_in.at[b], force_send, force_recv.at[b],
            device_id=device(-OFFSETS[b]), device_id_type=MESH,
        ).start()


    def both_halves(tile):
        return tile + pltpu.roll(tile, 4, 0)

    def send_round(s, elevation):
        for half in range(2):
            height[pl.ds(half * 8, 8), :] = elevation[half] + flux[pl.ds(96 + half * 8, 8), :]
        centre = list_values(lambda j: height[pl.ds(j, 1), :])
        first = jnp.zeros((8, 128), F32)
        second = jnp.zeros((8, 128), F32)
        for t in range(3):
            lane, block = list_lane[pl.ds(t * 8, 8), :], list_block[pl.ds(t * 8, 8), :]
            got = jnp.zeros((8, 128), F32)
            for j in range(BLOCKS):
                got = jnp.where(block == j, lane_pick(wide(height[pl.ds(j, 1), :]), lane), got)
            got = jnp.where(block < BLOCKS, got, centre)
            first = first + list_g[pl.ds(t * 8, 8), :] * (got - centre)
            second = second + list_g[pl.ds(24 + t * 8, 8), :] * (got - centre)
        first, second = both_halves(first), both_halves(second)
        sub = lax.broadcasted_iota(I32, (8, 128), 0)
        message[s, pl.ds(0, 8), :] = jnp.where(sub < 4, centre, first)
        message[s, pl.ds(8, 8), :] = second
        for ahead in (1, 0):
            for size in (2, 1, 3, 4):
                side = odd if ahead else 1 - odd
                to = device((2 * side - 1) * size)
                if size < 3:
                    pltpu.make_async_remote_copy(
                        message.at[s], near_box.at[s, 2 * (size - 1) + side], near_send, near_recv.at[s],
                        device_id=to, device_id_type=MESH,
                    ).start()
                else:
                    pltpu.make_async_remote_copy(
                        message.at[s, pl.ds(0, 8)], far_box.at[s, 2 * (size - 3) + side], far_send, far_recv.at[s],
                        device_id=to, device_id_type=MESH,
                    ).start()

    def own_sum(rows_of, centres):
        sums = [[jnp.zeros((8, 128), F32) for _ in range(2)] for _ in range(2)]
        for t in range(12):
            half, rows = t % 2, pl.ds(t * 8, 8)
            lane, block = own_lane[rows, :], own_block[rows, :]
            got = centres[half]
            for j, load in rows_of:
                got = jnp.where(block == j, lane_pick(load(), lane), got)
            apart = got - centres[half]
            for axis in range(2):
                weight = tab[pl.ds((G0 + 6 * axis) * 16 + t * 8, 8), :]
                sums[axis][half] = sums[axis][half] + weight * apart
        return sums

    def take_round(s, elevation, flow, ghost_flow, partial):
        def near(b, row):
            return wide(near_box[s, b, pl.ds(row, 1), :])

        def listed(distance, row):
            if distance == 0:
                return wide(message[s, pl.ds(row, 1), :])
            k = DISTANCES.index(distance)
            return near(k, row) if k < 4 else wide(far_box[s, k - 4, pl.ds(row, 1), :])

        which = lax.broadcasted_iota(I32, (8, 128), 0) & 3

        def by_list(load):
            out = load(0)
            for b in range(1, 4):
                out = jnp.where(which == b, load(b), out)
            return out

        centres = [height[pl.ds(half * 8, 8), :] for half in range(2)]
        rest = own_sum([(16 + b, lambda b=b: near(b, b)) for b in range(4)], centres)
        centre = by_list(lambda b: near(b, b))
        second_hand = [by_list(lambda b: listed(OFFSETS[b] + OFFSETS[j], j)) for j in range(4)]
        ghost_sums = [jnp.zeros((8, 128), F32) for _ in range(2)]
        for t in range(3):
            rows = pl.ds(t * 8, 8)
            lane, block = ghost_lane[rows, :], ghost_block[rows, :]
            got = centre
            for j in range(4):
                got = jnp.where(block == 16 + j, lane_pick(second_hand[j], lane), got)
            for axis in range(2):
                ghost_sums[axis] = ghost_sums[axis] + ghost_g[pl.ds(axis * 24 + t * 8, 8), :] * (got - centre)
        ghost_sums = [
            both_halves(ghost_sums[a]) + by_list(lambda b: near(b, 4 + 4 * a + b)) for a in range(2)
        ]

        turn = ghost_rows[pl.ds(0, 8), :]
        ghost_next = (
            ghost_flow[0] - ghost_sums[0] + turn * ghost_flow[1] + FORCE_GAIN * ghost_rows[pl.ds(8, 8), :],
            ghost_flow[1] - ghost_sums[1] - turn * ghost_flow[0] + FORCE_GAIN * ghost_rows[pl.ds(16, 8), :],
        )
        flow_next = []
        for half in range(2):
            turn = tab[pl.ds(COR * 16 + half * 8, 8), :]
            force = [tab[pl.ds((FORCE + a) * 16 + half * 8, 8), :] for a in range(2)]
            grad = [partial[a][half] + rest[a][half] for a in range(2)]
            flow_next.append(
                (
                    flow[half][0] - grad[0] + turn * flow[half][1] + FORCE_GAIN * force[0],
                    flow[half][1] - grad[1] - turn * flow[half][0] + FORCE_GAIN * force[1],
                )
            )
        for a in range(2):
            for half in range(2):
                speed[pl.ds(a * 24 + half * 8, 8), :] = flow_next[half][a]
            speed[pl.ds(a * 24 + 16, 8), :] = ghost_next[a]
        spread = [jnp.zeros((8, 128), F32) for _ in range(2)]
        for t in range(12):
            half, rows = t % 2, pl.ds(t * 8, 8)
            lane, block = own_lane[rows, :], own_block[rows, :]
            got = [jnp.zeros((8, 128), F32) for _ in range(2)]
            for j in range(20):
                here = block == j
                for a in range(2):
                    got[a] = jnp.where(here, lane_pick(wide(speed[pl.ds(a * 24 + j, 1), :]), lane), got[a])
            for a in range(2):
                weight = tab[pl.ds((G0 + 6 * a) * 16 + t * 8, 8), :]
                spread[half] = spread[half] + weight * (got[a] - flow_next[half][a])
        elevation_next = tuple(
            elevation[half] - spread[half] + FORCE_GAIN * flux[pl.ds(112 + half * 8, 8), :]
            for half in range(2)
        )
        return elevation_next, tuple(flow_next), ghost_next

    def sweep_up():
        def step(i, carry):
            index = LAYERS - 1 - i
            here, below = gain_here[layer(index), :], gain_below[layer(index), :]
            out = []
            for t in range(TRACERS):
                rows = layer(t * LAYERS + index)
                value = here * profile[rows, :] + below * carry[t]
                profile[rows, :] = value
                out.append(value)
            return tuple(out)

        zero = jnp.zeros((16, 128), F32)
        return lax.fori_loop(0, LAYERS - 2, step, (zero,) * TRACERS)

    def zero_state():
        elevation = tuple(surface[pl.ds(half * 8, 8), :] for half in range(2))
        flow = tuple(
            tuple(tab[pl.ds((VEL + a) * 16 + half * 8, 8), :] for a in range(2)) for half in range(2)
        )
        return elevation, flow

    def one_round(s, state, work):
        elevation, flow, ghost_flow = state
        centres = [height[pl.ds(half * 8, 8), :] for half in range(2)]
        own_rows = [(j, lambda j=j: wide(height[pl.ds(j, 1), :])) for j in range(16)]
        partial = own_sum(own_rows, centres)
        work()
        pltpu.make_async_copy(far_box.at[s], far_box.at[s], far_recv.at[s]).wait()
        pltpu.make_async_copy(near_box.at[s], near_box.at[s], near_recv.at[s]).wait()

        @pl.when(s == 0)
        def _():
            for b in range(4):
                pltpu.make_async_copy(force_in.at[b], force_in.at[b], force_recv.at[b]).wait()
                for a in range(2):
                    for copy in range(2):
                        row = force_in[b, pl.ds(a * 4 + b, 1), :]
                        ghost_rows[pl.ds(8 + a * 8 + copy * 4 + b, 1), :] = row

        return take_round(s, elevation, flow, ghost_flow, partial)

    elevation, flow = zero_state()
    send_round(0, elevation)
    pltpu.make_async_copy(ghost_fixed, ghost_fixed, fixed_recv).wait()
    by_edge(ghost_fixed, ghost_lane, ghost_block, ghost_g)
    for b in range(4):
        for copy in range(2):
            for row, field in ((0, COR), (24, VEL), (32, VEL + 1)):
                ghost_rows[pl.ds(row + copy * 4 + b, 1), :] = ghost_fixed[pl.ds(b * FIXED + field, 1), :]
    ghost_flow = (ghost_rows[pl.ds(24, 8), :], ghost_rows[pl.ds(32, 8), :])

    def split_halo():
        pltpu.make_async_copy(halo_in, halo_in, halo_recv).wait()
        for b in range(4):
            value = halo_in[b]
            high = value.astype(BF16)
            halo_parts[pl.ds(0, ROWS), pl.ds(b * 128, 128)] = high
            halo_parts[pl.ds(ROWS, ROWS), pl.ds(b * 128, 128)] = (value - high.astype(F32)).astype(BF16)

    def sweep_down(index, carry):
        above = gain_above[layer(index), :]
        share = above * carry[0]
        gain_above[layer(index), :] = share
        out = []
        for t in range(TRACERS):
            rows = layer(t * LAYERS + index)
            value = profile[rows, :] + above * carry[1 + t]
            profile[rows, :] = value
            out.append(value)
        return (share, *out)

    def place_out(c, carry):
        cells = pl.ds(pl.multiple_of(c * 128, 128), 128)
        deep = lax.broadcasted_iota(I32, (8, 128), 0) > 1
        for g in range(ROWS // 8):
            value = profile[pl.ds(g * 128 + c, 8, stride=16), :]
            if g % 8 == 0:
                value = jnp.where(deep, value, 0.0)
            total[pl.ds(g * 8, 8), cells] = value
        for g in range(LAYERS // 8):
            thick[pl.ds(g * 8, 8), cells] = gain_above[pl.ds(g * 128 + c, 8, stride=16), :]
        return carry

    stores = (
        pltpu.make_async_copy(total, rest_hbm, store_sem.at[0]),
        pltpu.make_async_copy(thick, share_hbm, store_sem.at[1]),
    )

    def solve_below():
        values = sweep_up()
        for t in range(TRACERS):
            tops[pl.ds(t * 16, 16), :] = values[t]
        zero, one = jnp.zeros((16, 128), F32), jnp.ones((16, 128), F32)
        gain_above[layer(0), :] = zero
        gain_above[layer(1), :] = one
        lax.fori_loop(2, LAYERS, sweep_down, (one,) + (zero,) * TRACERS)
        lax.fori_loop(0, BLOCKS, place_out, 0)
        for store in stores:
            store.start()

    def tracer_work(s):
        @pl.when(s == 0)
        def _():
            select_halo()

        @pl.when(s < 4)
        def _():
            send_halo(s)

        @pl.when(jnp.logical_and(s >= 1, s < 5))
        def _():
            def step(i, carry):
                mix_own(2 * (s - 1) + i)
                return carry

            lax.fori_loop(0, 2, step, 0)

        @pl.when(s == 5)
        def _():
            split_halo()
            remap(0)

        @pl.when(jnp.logical_and(s >= 5, s < 7))
        def _():
            def step(i, carry):
                mix_halo(4 * (s - 5) + i)
                return carry

            lax.fori_loop(0, 4, step, 0)

        @pl.when(s == 7)
        def _():
            solve_below()

    def subcycle(s, state):
        state = one_round(s, state, lambda: tracer_work(s))

        @pl.when(s < SUBCYCLES - 1)
        def _():
            send_round(s + 1, state[0])

        return state

    elevation, flow, ghost_flow = lax.fori_loop(0, SUBCYCLES, subcycle, (elevation, flow, ghost_flow))

    for half in range(2):
        final_surface[pl.ds(half * 8, 8), :] = elevation[half]
    for c in range(BLOCKS):
        final_velocity[0:1, pl.ds(c * 128, 128)] = speed[pl.ds(c, 1), :]
        final_velocity[1:2, pl.ds(c * 128, 128)] = speed[pl.ds(24 + c, 1), :]

    top = thick_cells[layer(0), :] + jnp.tanh(final_surface[...])
    second = thick_cells[layer(1), :]
    couple_zero = couple(0, top)
    inverse_one = 1.0 / (second + couple_zero + couple_one - couple_one * gain_two)
    gain_one = couple_zero * inverse_one
    inverse_zero = 1.0 / (top + couple_zero - couple_zero * gain_one)
    for t in range(TRACERS):
        rows_zero, rows_one = layer(t * LAYERS), layer(t * LAYERS + 1)
        value_one = (second * profile[rows_one, :] + couple_one * tops[pl.ds(t * 16, 16), :]) * inverse_one
        right = top * profile[rows_zero, :] + FLUX_GAIN * flux[pl.ds(t * 16, 16), :]
        value_zero = (right + couple_zero * value_one) * inverse_zero
        square[pl.ds(t * 16, 16), :] = value_zero
        square[pl.ds(64 + t * 16, 16), :] = value_one + gain_one * value_zero
    for c in range(BLOCKS):
        heads[:, pl.ds(c * 128, 128)] = square[pl.ds(c, 8, stride=16), :]

    for store in stores:
        store.wait()
    pltpu.make_async_copy(near_box, near_box, near_send).wait()
    pltpu.make_async_copy(far_box, far_box, far_send).wait()
    pltpu.make_async_copy(list_fixed, list_fixed, fixed_send).wait()
    pltpu.make_async_copy(force_in, force_in, force_send).wait()
    pltpu.make_async_copy(halo_out, halo_out, halo_send_sem).wait()
    pltpu.make_async_copy(gathered, gathered, col_send).wait()
    pltpu.make_async_copy(arrived.at[others], arrived.at[others], ocn_send).wait()


def finish_kernel(
    rest_hbm, share_hbm, heads_hbm, surface_hbm, flow_hbm, mixed_hbm, surface_out, flow_out,
    rest, share, heads, load_sem, store_sem,
):
    loads = [
        pltpu.make_async_copy(share_hbm, share, load_sem.at[0]),
        pltpu.make_async_copy(heads_hbm, heads, load_sem.at[1]),
    ]
    stores = [
        pltpu.make_async_copy(surface_hbm, surface_out, store_sem.at[0]),
        pltpu.make_async_copy(flow_hbm, flow_out, store_sem.at[1]),
    ]
    pieces = [pl.ds(start, PIECE) for start in range(0, ROWS, PIECE)]
    for i, rows in enumerate(pieces):
        loads.append(pltpu.make_async_copy(rest_hbm.at[rows], rest.at[rows], load_sem.at[2 + i]))
        stores.append(pltpu.make_async_copy(rest.at[rows], mixed_hbm.at[rows], store_sem.at[2 + i]))
    for copy in loads + stores[:2]:
        copy.start()
    loads[0].wait()
    loads[1].wait()
    sub = lax.broadcasted_iota(I32, (8, 2048), 0)
    for i in range(len(pieces)):
        loads[2 + i].wait()
        t = i * PIECE // LAYERS
        head = jnp.broadcast_to(heads[pl.ds(4 + t, 1), :], (8, 2048))
        for first in range(i * PIECE, (i + 1) * PIECE, 8):
            rows = pl.ds(first, 8)
            value = rest[rows, :] + share[pl.ds(first % LAYERS, 8), :] * head
            if first % LAYERS == 0:
                value = jnp.where(sub == 0, jnp.broadcast_to(heads[pl.ds(t, 1), :], (8, 2048)), value)
            rest[rows, :] = value
        stores[2 + i].start()
    for store in stores:
        store.wait()


def finish(*operands):
    hbm = pl.BlockSpec(memory_space=pl.ANY)
    return pl.pallas_call(
        finish_kernel,
        name="finish",
        out_shape=(
            jax.ShapeDtypeStruct((ROWS, 2048), F32),
            jax.ShapeDtypeStruct((16, 128), F32),
            jax.ShapeDtypeStruct((2, 2048), F32),
        ),
        in_specs=[hbm] * 5,
        out_specs=(hbm,) * 3,
        scratch_shapes=[
            pltpu.VMEM((ROWS, 2048), F32),
            pltpu.VMEM((LAYERS, 2048), F32),
            pltpu.VMEM((8, 2048), F32),
            pltpu.SemaphoreType.DMA((2 + ROWS // PIECE,)),
            pltpu.SemaphoreType.DMA((2 + ROWS // PIECE,)),
        ],
        compiler_params=pltpu.CompilerParams(vmem_limit_bytes=60 << 20),
    )(*operands)


def ocean(ocn_size, col_size, *operands):
    vmem = pl.BlockSpec(memory_space=pltpu.VMEM)
    hbm = pl.BlockSpec(memory_space=pl.ANY)

    def kernel(*refs):
        ocean_kernel(ocn_size, col_size, *refs)

    scratch = [
        pltpu.VMEM((8, 2048), F32),
        pltpu.VMEM((16, 128), I32),
        pltpu.VMEM((4, 2048), I32),
        pltpu.VMEM((4, 2048), F32),
        pltpu.VMEM((1, 4, 128), I32),
        pltpu.VMEM((EDGES, 2048), I32),
        pltpu.VMEM((EDGES, 2, 2048), F32),
        pltpu.VMEM((16, 128), F32),
        pltpu.VMEM((16, 128), F32),
        pltpu.VMEM((2, 2048), F32),
        pltpu.VMEM((EDGES, 2048), F32),
        pltpu.VMEM((16, 128), I32),
        pltpu.VMEM((LAYERS, 2048), F32),
        pltpu.VMEM((LAYERS - 1, 2048), F32),
        pltpu.VMEM((ROWS, 2048), F32),
        pltpu.VMEM((FIXED * 16, 128), F32),
        pltpu.VMEM((128, 128), F32),
        pltpu.VMEM((ocn_size // 2, 2 * col_size, 1, 128), F32),
        pltpu.VMEM((2 * col_size, ocn_size // 2, 1, 128), F32),
        pltpu.VMEM((ocn_size * col_size, 1, 128), F32),
        pltpu.VMEM((16, 8, 128), F32),
        pltpu.VMEM((16, 8, 128), F32),
        pltpu.VMEM((128, 128), F32),
        pltpu.VMEM((4 * FIXED, 128), F32),
        pltpu.VMEM((4 * FIXED, 128), F32),
        pltpu.VMEM((8, 128), F32),
        pltpu.VMEM((4, 8, 128), F32),
        pltpu.VMEM((96, 128), I32),
        pltpu.VMEM((96, 128), I32),
        pltpu.VMEM((24, 128), I32),
        pltpu.VMEM((24, 128), I32),
        pltpu.VMEM((48, 128), F32),
        pltpu.VMEM((24, 128), I32),
        pltpu.VMEM((24, 128), I32),
        pltpu.VMEM((48, 128), F32),
        pltpu.VMEM((16, 128), F32),
        pltpu.VMEM((48, 128), F32),
        pltpu.VMEM((40, 128), F32),
        pltpu.VMEM((SUBCYCLES, 16, 128), F32),
        pltpu.VMEM((SUBCYCLES, 4, 16, 128), F32),
        pltpu.VMEM((SUBCYCLES, 4, 8, 128), F32),
        pltpu.VMEM((4, ROWS, 128), F32),
        pltpu.VMEM((4, ROWS, 128), F32),
        pltpu.VMEM((2 * ROWS, 2048), BF16),
        pltpu.VMEM((2 * ROWS, 512), BF16),
        pltpu.VMEM((ROWS, 2048), F32),
        pltpu.VMEM((ROWS * 16, 128), F32),
        pltpu.VMEM((LAYERS * 16, 128), F32),
        pltpu.VMEM((LAYERS * 16, 128), F32),
        pltpu.VMEM((LAYERS * 16, 128), F32),
        pltpu.VMEM((LAYERS * 16, 128), F32),
        pltpu.VMEM((LAYERS * 16, 128), F32),
        pltpu.VMEM((TRACERS * 16, 128), F32),
        pltpu.SemaphoreType.DMA((15,)),
        pltpu.SemaphoreType.DMA((2,)),
        pltpu.SemaphoreType.DMA,
        pltpu.SemaphoreType.DMA,
        pltpu.SemaphoreType.DMA,
        pltpu.SemaphoreType.DMA,
        pltpu.SemaphoreType.DMA,
        pltpu.SemaphoreType.DMA,
        pltpu.SemaphoreType.DMA,
        pltpu.SemaphoreType.DMA,
        pltpu.SemaphoreType.DMA,
        pltpu.SemaphoreType.DMA((4,)),
        pltpu.SemaphoreType.DMA,
        pltpu.SemaphoreType.DMA,
        pltpu.SemaphoreType.DMA,
        pltpu.SemaphoreType.DMA((SUBCYCLES,)),
        pltpu.SemaphoreType.DMA,
        pltpu.SemaphoreType.DMA((SUBCYCLES,)),
    ]
    return pl.pallas_call(
        kernel,
        name="ocean",
        out_shape=(
            jax.ShapeDtypeStruct((ROWS, 2048), F32),
            jax.ShapeDtypeStruct((LAYERS, 2048), F32),
            jax.ShapeDtypeStruct((8, 2048), F32),
            jax.ShapeDtypeStruct((16, 128), F32),
            jax.ShapeDtypeStruct((2, 2048), F32),
        ),
        in_specs=[hbm] * 15,
        out_specs=(hbm, hbm, vmem, vmem, vmem),
        scratch_shapes=scratch,
        compiler_params=pltpu.CompilerParams(
            collective_id=0, has_side_effects=True, vmem_limit_bytes=60 << 20
        ),
    )(*operands)


def solution(mesh):
    ocn_size, col_size = mesh.shape["ocn"], mesh.shape["col"]

    def per_device(
        air_flux,
        send_index,
        remap_column,
        remap_weight,
        halo_send,
        neighbours,
        gradient_weight,
        coriolis,
        sea_surface,
        velocity,
        lateral_weight,
        layer_count,
        thickness,
        diffusivity,
        tracers,
    ):
        solved = ocean(
            ocn_size,
            col_size,
            air_flux,
            send_index[0].T,
            remap_column,
            remap_weight,
            halo_send,
            neighbours,
            jnp.swapaxes(gradient_weight, 0, 1),
            coriolis.reshape(16, 128),
            sea_surface.reshape(16, 128),
            velocity,
            lateral_weight,
            layer_count.reshape(16, 128),
            thickness,
            diffusivity,
            tracers.reshape(ROWS, 2048),
        )
        mixed, elevation, flow = finish(*solved)
        return mixed.reshape(TRACERS, LAYERS, 2048), elevation.reshape(2048), flow

    both = ("ocn", "col")
    placed = (
        P(None, both),
        P(both, None, None),
        P(None, both),
        P(None, both),
        P(both, None, None),
        P(None, both),
        P(None, None, both),
        P(both),
        P(both),
        P(None, both),
        P(None, both),
        P(both),
        P(None, both),
        P(None, both),
        P(None, None, both),
    )
    return jax.shard_map(
        per_device,
        mesh=mesh,
        in_specs=placed,
        out_specs=(P(None, None, both), P(both), P(None, both)),
        check_vma=False,
    )
```

profile of v0, /device:TPU:0, one launch (start us, length us, event | category | flops | bytes accessed | tf_op | source)
XLA Modules:
  0.0 70.3 jit_solution(7688426964223055970)
XLA Ops:
  0.6 67.0 %ocean.1 = (f32[256,2048]{1,0:T(8,128)}, f32[64,2048]{1,0:T(8,128)}, f32[8,2048]{1,0:T(8,128)}, f32[16,128]{1,0:T(8,128)}, f32[2,2048]{1,0:T(2,128)}) custom-call(f32[8,2048]{1,0:T(8,128)} %refs_0_.1, s32[16,128]{1,0:T(8,128)} %bitcast.12, s32[4,2048]{1,0:T(4,128)} %refs_2_.1, f32[4,2048]{1,0:T(4,128)} %refs_3_.1, s32[1,4,128]{2,1,0:T(4,128)} %refs_4_.1, ...), custom_call_target="tpu_custom_call" | custom-call | tf_op jit(solution)/shard_map/ocean/pallas_call | solution.py:871
  67.6 2.6 %finish.1 = (f32[256,2048]{1,0:T(8,128)}, f32[16,128]{1,0:T(8,128)}, f32[2,2048]{1,0:T(2,128)}) custom-call(f32[256,2048]{1,0:T(8,128)} %get-tuple-element.11.rest_hbm, f32[64,2048]{1,0:T(8,128)} %get-tuple-element.12.share_hbm, f32[8,2048]{1,0:T(8,128)} %get-tuple-element.13.heads_hbm, f32[16,128]{1,0:T(8,128)} %get-tuple-element.14.surface_hbm, ...), custom_call_target="tpu_custom_call" | custom-call | tf_op jit(solution)/shard_map/finish/pallas_call | solution.py:770
where the time goes:
time: 70.4 us; the launch traced here: 70.3 us
  Pallas kernels  69.6 us (99%)
    pallas_call x1, Pallas kernels, ocean(): pl.pallas_call(kernel, name='ocean', out_shape=(jax.ShapeDtypeStruct((ROW...  67 us
    pallas_call x1, Pallas kernels, finish(): pl.pallas_call(finish_kernel, name='finish', out_shape=(jax.ShapeDtypeStr...  2.64 us

commit v1 on v0

--- a/solution.py
+++ b/solution.py
@@ -167,12 +167,12 @@
         load.start()
 
     barrier = pltpu.get_barrier_semaphore()
+    for step in range(1, chips):
+        pl.semaphore_signal(barrier, inc=1, device_id=across(step)[1], device_id_type=MESH)
     for distance in DISTANCES:
         pl.semaphore_signal(barrier, inc=1, device_id=device(distance), device_id_type=MESH)
     for step in range(1, column_size):
         pl.semaphore_signal(barrier, inc=1, device_id=in_column(step)[1], device_id_type=MESH)
-    for step in range(1, chips):
-        pl.semaphore_signal(barrier, inc=1, device_id=across(step)[1], device_id_type=MESH)
     for load in loads[2:]:
         load.start()
 
@@ -444,22 +444,23 @@
             got = jnp.where(block < BLOCKS, got, centre)
             first = first + list_g[pl.ds(t * 8, 8), :] * (got - centre)
             second = second + list_g[pl.ds(24 + t * 8, 8), :] * (got - centre)
-        first, second = both_halves(first), both_halves(second)
+        first = both_halves(first)
+        second = pltpu.roll(second, 1, 0) + pltpu.roll(second, 5, 0)
         sub = lax.broadcasted_iota(I32, (8, 128), 0)
-        message[s, pl.ds(0, 8), :] = jnp.where(sub < 4, centre, first)
-        message[s, pl.ds(8, 8), :] = second
+        for b in range(4):
+            message[s, b, :, :] = jnp.where(sub < 4, centre, jnp.where(sub == 4 + b, first, second))
         for ahead in (1, 0):
             for size in (2, 1, 3, 4):
                 side = odd if ahead else 1 - odd
                 to = device((2 * side - 1) * size)
                 if size < 3:
                     pltpu.make_async_remote_copy(
-                        message.at[s], near_box.at[s, 2 * (size - 1) + side], near_send, near_recv.at[s],
+                        message.at[s, 2 * (size - 1) + side], near_box.at[s, 2 * (size - 1) + side], near_send, near_recv.at[s],
                         device_id=to, device_id_type=MESH,
                     ).start()
                 else:
                     pltpu.make_async_remote_copy(
-                        message.at[s, pl.ds(0, 8)], far_box.at[s, 2 * (size - 3) + side], far_send, far_recv.at[s],
+                        message.at[s, 0], far_box.at[s, 2 * (size - 3) + side], far_send, far_recv.at[s],
                         device_id=to, device_id_type=MESH,
                     ).start()
 
@@ -483,7 +484,7 @@
 
         def listed(distance, row):
             if distance == 0:
-                return wide(message[s, pl.ds(row, 1), :])
+                return wide(message[s, 0, pl.ds(row, 1), :])
             k = DISTANCES.index(distance)
             return near(k, row) if k < 4 else wide(far_box[s, k - 4, pl.ds(row, 1), :])
 
@@ -509,7 +510,7 @@
             for axis in range(2):
                 ghost_sums[axis] = ghost_sums[axis] + ghost_g[pl.ds(axis * 24 + t * 8, 8), :] * (got - centre)
         ghost_sums = [
-            both_halves(ghost_sums[a]) + by_list(lambda b: near(b, 4 + 4 * a + b)) for a in range(2)
+            both_halves(ghost_sums[a]) + by_list(lambda b: near(b, 4 + (b + a) % 4)) for a in range(2)
         ]
 
         turn = ghost_rows[pl.ds(0, 8), :]
@@ -834,8 +835,8 @@
         pltpu.VMEM((16, 128), F32),
         pltpu.VMEM((48, 128), F32),
         pltpu.VMEM((40, 128), F32),
-        pltpu.VMEM((SUBCYCLES, 16, 128), F32),
-        pltpu.VMEM((SUBCYCLES, 4, 16, 128), F32),
+        pltpu.VMEM((SUBCYCLES, 4, 8, 128), F32),
+        pltpu.VMEM((SUBCYCLES, 4, 8, 128), F32),
         pltpu.VMEM((SUBCYCLES, 4, 8, 128), F32),
         pltpu.VMEM((4, ROWS, 128), F32),
         pltpu.VMEM((4, ROWS, 128), F32),

time: 70.4 us -> 69.6 us (0.989)
  Pallas kernels: 69.6 us -> 68.8 us
    pallas_call x1, Pallas kernels: 67 us -> 66.2 us  [ocean(): pl.pallas_call(kernel, name='ocean', out_shape=(jax.ShapeDtypeStruct((ROW...]
where the time goes in v1:
time: 69.6 us; the launch traced here: 69.5 us
  Pallas kernels  68.8 us (99%)
    pallas_call x1, Pallas kernels, ocean(): pl.pallas_call(kernel, name='ocean', out_shape=(jax.ShapeDtypeStruct((ROW...  66.2 us
    pallas_call x1, Pallas kernels, finish(): pl.pallas_call(finish_kernel, name='finish', out_shape=(jax.ShapeDtypeStr...  2.64 us

profile of v1, /device:TPU:0, one launch (start us, length us, event | category | flops | bytes accessed | tf_op | source)
XLA Modules:
  0.0 69.5 jit_solution(12762238536641227780)
XLA Ops:
  0.6 66.2 %ocean.1 = (f32[256,2048]{1,0:T(8,128)}, f32[64,2048]{1,0:T(8,128)}, f32[8,2048]{1,0:T(8,128)}, f32[16,128]{1,0:T(8,128)}, f32[2,2048]{1,0:T(2,128)}) custom-call(f32[8,2048]{1,0:T(8,128)} %refs_0_.1, s32[16,128]{1,0:T(8,128)} %bitcast.12, s32[4,2048]{1,0:T(4,128)} %refs_2_.1, f32[4,2048]{1,0:T(4,128)} %refs_3_.1, s32[1,4,128]{2,1,0:T(4,128)} %refs_4_.1, ...), custom_call_target="tpu_custom_call" | custom-call | tf_op jit(solution)/shard_map/ocean/pallas_call | solution.py:872
  66.8 2.6 %finish.1 = (f32[256,2048]{1,0:T(8,128)}, f32[16,128]{1,0:T(8,128)}, f32[2,2048]{1,0:T(2,128)}) custom-call(f32[256,2048]{1,0:T(8,128)} %get-tuple-element.11.rest_hbm, f32[64,2048]{1,0:T(8,128)} %get-tuple-element.12.share_hbm, f32[8,2048]{1,0:T(8,128)} %get-tuple-element.13.heads_hbm, f32[16,128]{1,0:T(8,128)} %get-tuple-element.14.surface_hbm, ...), custom_call_target="tpu_custom_call" | custom-call | tf_op jit(solution)/shard_map/finish/pallas_call | solution.py:771
